TPU v7x, 512 devices: a whole 4x8x8 slice. The times are simulated.
512 devices in a mesh: dp: 8 (over z), expert: 64 (over x, y, core).
Axes of the slice: x: 4, y: 8, z: 8, core: 2. Of those that a mesh axis runs over, the one named last changes fastest.
Arguments:
- tokens: bfloat16 [65536, 1024], P(('dp', 'expert')), may hold values from -6 to 6
- cotangent: bfloat16 [65536, 1024], P(('dp', 'expert')), may hold values from -6 to 6
- routes: int32 [65536, 8], P(('dp', 'expert')), may hold values from 0 to 63, as said below
- combine: float32 [65536, 8], P(('dp', 'expert')), may hold values from 0.1 to 0.5
- w_gate: bfloat16 [64, 1024, 384], P('expert', 'dp'), may hold values from -0.1875 to 0.1875
- w_up: bfloat16 [64, 1024, 384], P('expert', 'dp'), may hold values from -0.1875 to 0.1875
- w_down: bfloat16 [64, 384, 1024], P('expert', None, 'dp'), may hold values from -0.3125 to 0.3125
Outputs:
- mixed: bfloat16 [65536, 1024], P(('dp', 'expert'))
- input_grad: bfloat16 [65536, 1024], P(('dp', 'expert'))
- combine_grad: float32 [65536, 8], P(('dp', 'expert'))
Inputs may be any that keep to these rules, and one draw needn't show every extreme that they name: `routes`: each row names 8 different experts. Among the rows of one device (aligned blocks of 128 rows) each of 2 frequent experts, the same ones on every device, is named by 48 to 56 rows, and every other expert by at most 15 rows, with the counts of the other experts on one device differing by at most one. In every draw some device has a frequent expert named by exactly 56 rows and some device an other expert named by exactly 15 rows.
All inputs are finite; a program needn't handle non-finite values.
Results may differ from a plain program's by a relative error of at most 0.017.
Values may be sent and summed in bfloat16 or wider, within the bound.
No kernel may reach another device: no remote copies, remote signals or barrier semaphores. Data moves between devices by JAX's collectives and lax.ppermute only.
A program may use at most 128 MiB of HBM per device.

v0:
```python
import jax
import jax.numpy as jnp
from jax import lax
from jax.sharding import PartitionSpec as P

HOT = 2


def broadcast(block, axis, owner):
    block = jnp.where(lax.axis_index(axis) == owner, block, jnp.zeros_like(block))
    return lax.psum(block, axis)


def to_owner(array, owners, local_count):
    shape = array.shape
    grouped = array.reshape((owners, local_count) + shape[1:])
    grouped = jnp.swapaxes(grouped, 0, 1)
    return grouped.reshape((local_count, owners * shape[1]) + shape[2:])


def from_owner(array, owners, local_count):
    shape = array.shape
    grouped = array.reshape((local_count, owners, shape[1] // owners) + shape[2:])
    grouped = jnp.swapaxes(grouped, 0, 1)
    return grouped.reshape((owners * local_count, shape[1] // owners) + shape[2:])


def expert_block(row_x, row_dy, row_g, w_g, w_u, w_d):
    gate_pre = jnp.einsum("erd,edf->erf", row_x, w_g, preferred_element_type=jnp.float32)
    up_proj = jnp.einsum("erd,edf->erf", row_x, w_u, preferred_element_type=jnp.float32)
    sigmoid_val = jax.nn.sigmoid(gate_pre)
    silu_val = gate_pre * sigmoid_val
    hidden = (silu_val * up_proj).astype(jnp.bfloat16)
    expert_out = jnp.einsum("erf,efd->erd", hidden, w_d, preferred_element_type=jnp.float32).astype(
        jnp.bfloat16
    )
    dot_grad = jnp.einsum("erd,efd->erf", row_dy, w_d, preferred_element_type=jnp.float32)
    hidden_grad = row_g[:, :, None] * dot_grad
    gate_grad = (
        hidden_grad * up_proj * sigmoid_val * (1.0 + gate_pre * (1.0 - sigmoid_val))
    ).astype(jnp.bfloat16)
    up_grad = (hidden_grad * silu_val).astype(jnp.bfloat16)
    row_grad = jnp.einsum("erf,edf->erd", gate_grad, w_g, preferred_element_type=jnp.float32)
    row_grad = (
        row_grad + jnp.einsum("erf,edf->erd", up_grad, w_u, preferred_element_type=jnp.float32)
    ).astype(jnp.bfloat16)
    return (expert_out, row_grad)


def on_device(tokens, cotangent, routes, combine, w_gate, w_up, w_down):
    tok_rows, width = tokens.shape
    topk = routes.shape[1]
    owners = lax.axis_size("expert")
    local_count = w_gate.shape[0]
    experts = local_count * owners
    pairs = tok_rows * topk
    hot_most = min(tok_rows, 7 * pairs // (2 * experts))
    hot_least = min(tok_rows * 3 // 4, 3 * pairs // experts)
    capacity = (pairs - HOT * hot_least + experts - HOT - 1) // (experts - HOT)
    cold_rows = experts * capacity
    pool_rows = cold_rows + HOT * hot_most
    expert_ids = routes.reshape(-1)
    one_hot = (expert_ids[:, None] == jnp.arange(experts, dtype=jnp.int32)[None, :]).astype(
        jnp.int32
    )
    rank_in = jnp.sum((jnp.cumsum(one_hot, axis=0) - 1) * one_hot, axis=1)
    counts = jnp.sum(one_hot, axis=0)
    top_counts, top_ids = lax.top_k(counts, HOT)
    hot_list = jnp.sort(top_ids)
    match = expert_ids[:, None] == hot_list[None, :]
    is_hot = jnp.any(match, axis=1)
    hot_rank = (
        jnp.sum(jnp.where(match, jnp.arange(HOT, dtype=jnp.int32)[None, :] * hot_most, 0), axis=1)
        + rank_in
    )
    slot_index = jnp.where(is_hot, cold_rows + hot_rank, expert_ids * capacity + rank_in)
    token_index = jnp.arange(pairs, dtype=jnp.int32) // topk
    source_token = jnp.full((pool_rows,), tok_rows, jnp.int32).at[slot_index].set(token_index)
    source_pair = (
        jnp.full((pool_rows,), pairs, jnp.int32)
        .at[slot_index]
        .set(jnp.arange(pairs, dtype=jnp.int32))
    )
    pool_x = jnp.take(tokens, source_token, axis=0, mode="fill", fill_value=0)
    pool_dy = jnp.take(cotangent, source_token, axis=0, mode="fill", fill_value=0)
    pool_g = jnp.take(combine.reshape(-1), source_pair, axis=0, mode="fill", fill_value=0)
    send_x = pool_x[:cold_rows].reshape(experts, capacity, width)
    send_dy = pool_dy[:cold_rows].reshape(experts, capacity, width)
    send_g = pool_g[:cold_rows].reshape(experts, capacity)
    hot_x = pool_x[cold_rows:].reshape(HOT, hot_most, width)
    hot_dy = pool_dy[cold_rows:].reshape(HOT, hot_most, width)
    hot_g = pool_g[cold_rows:].reshape(HOT, hot_most)
    recv_x, recv_dy, recv_g = (
        lax.all_to_all(send_x, "expert", split_axis=0, concat_axis=0, tiled=True),
        lax.all_to_all(send_dy, "expert", split_axis=0, concat_axis=0, tiled=True),
        lax.all_to_all(
            send_g.astype(jnp.bfloat16), "expert", split_axis=0, concat_axis=0, tiled=True
        ).astype(send_g.dtype),
    )
    full_gate, full_up, full_down = (
        lax.all_gather(w_gate, "dp", axis=1, tiled=True),
        lax.all_gather(w_up, "dp", axis=1, tiled=True),
        lax.all_gather(w_down, "dp", axis=2, tiled=True),
    )
    gate_list = []
    up_list = []
    down_list = []
    for which in range(HOT):
        root = hot_list[which] // local_count
        local_slot = hot_list[which] % local_count
        piece_gate = lax.dynamic_index_in_dim(w_gate, local_slot, 0, keepdims=False)
        piece_up = lax.dynamic_index_in_dim(w_up, local_slot, 0, keepdims=False)
        piece_down = lax.dynamic_index_in_dim(w_down, local_slot, 0, keepdims=False)
        shard_gate, shard_up, shard_down = (
            broadcast(piece_gate, "expert", root),
            broadcast(piece_up, "expert", root),
            broadcast(piece_down, "expert", root),
        )
        got_gate, got_up, got_down = (
            lax.all_gather(shard_gate, "dp", axis=0, tiled=True),
            lax.all_gather(shard_up, "dp", axis=0, tiled=True),
            lax.all_gather(shard_down, "dp", axis=1, tiled=True),
        )
        gate_list.append(got_gate)
        up_list.append(got_up)
        down_list.append(got_down)
    hot_out, hot_grad = expert_block(
        hot_x, hot_dy, hot_g, jnp.stack(gate_list), jnp.stack(up_list), jnp.stack(down_list)
    )
    row_x = to_owner(recv_x, owners, local_count)
    row_dy = to_owner(recv_dy, owners, local_count)
    row_g = to_owner(recv_g, owners, local_count)
    expert_out, row_grad = expert_block(row_x, row_dy, row_g, full_gate, full_up, full_down)
    back_out, back_grad = (
        lax.all_to_all(
            from_owner(expert_out, owners, local_count),
            "expert",
            split_axis=0,
            concat_axis=0,
            tiled=True,
        ),
        lax.all_to_all(
            from_owner(row_grad, owners, local_count),
            "expert",
            split_axis=0,
            concat_axis=0,
            tiled=True,
        ),
    )
    pool_out = jnp.concatenate(
        [back_out.reshape(cold_rows, width), hot_out.reshape(HOT * hot_most, width)], axis=0
    )
    pool_grad = jnp.concatenate(
        [back_grad.reshape(cold_rows, width), hot_grad.reshape(HOT * hot_most, width)], axis=0
    )
    out_pairs = pool_out[slot_index].reshape(tok_rows, topk, width)
    grad_pairs = pool_grad[slot_index].reshape(tok_rows, topk, width)
    mixed = jnp.einsum("tk,tkd->td", combine, out_pairs.astype(jnp.float32)).astype(jnp.bfloat16)
    input_grad = jnp.sum(grad_pairs.astype(jnp.float32), axis=1).astype(jnp.bfloat16)
    combine_grad = jnp.einsum(
        "tkd,td->tk", out_pairs, cotangent, preferred_element_type=jnp.float32
    )
    return (mixed, input_grad, combine_grad)


def solution(mesh):
    placed = (
        P(("dp", "expert"), None),
        P(("dp", "expert"), None),
        P(("dp", "expert"), None),
        P(("dp", "expert"), None),
        P("expert", "dp", None),
        P("expert", "dp", None),
        P("expert", None, "dp"),
    )
    return jax.shard_map(
        on_device,
        mesh=mesh,
        in_specs=placed,
        out_specs=(P(("dp", "expert"), None), P(("dp", "expert"), None), P(("dp", "expert"), None)),
        check_vma=False,
    )
```

profile of v0, /device:TPU:22, one launch (start us, length us, event | category | flops | bytes accessed | tf_op | source)
XLA Modules:
  0.0 678.3 jit_solution(17495965251228169367)
XLA Ops:
  10.0 18.0 %reduce-window.6 = s32[64,8,128]{2,1,0:T(8,128)S(1)} reduce-window(s32[64,8,128]{2,1,0:T(8,128)S(1)} %fusion.22, s32[]{:T(128)} %constant.105.clone.1), window={size=1x1x128 pad=0_0x0_0x127_0}, to_apply=%region_5.6 | reduce-window | flops 8323072 | bytes 524292 | tf_op jit(solution)/shard_map/reduce-window
  28.7 2.0 top_k.11
  31.9 4.3 scatter_custom_fusion.1
  36.2 4.4 gather_fusion.1
  41.4 10.6 %all-to-all-start.2 = ((bf16[64,1,15]{2,1,0:T(2,128)(2,1)}), bf16[64,1,15]{2,1,0:T(2,128)(2,1)S(1)}, u32[]{:S(2)}, u32[]{:S(2)}) async-start(bf16[64,1,15]{2,1,0:T(2,128)(2,1)} %convert_element_type.86), calls=%async_computation.2 | async-start | bytes 65536 | tf_op jit(solution)/shard_map/all_to_all | solution.py:96
  52.0 4.3 scatter_custom_fusion
  56.4 4.4 gather_fusion.4
  60.8 4.9 gather_fusion.3
  65.7 3.3 broadcast_select_fusion
  69.1 1.4 copy-done.2
  70.6 1.7 reshape.219
  72.9 10.6 %all-to-all-start = ((bf16[64,15,1024]{2,1,0:T(8,128)(2,1)}), bf16[64,15,1024]{2,1,0:T(8,128)(2,1)}, u32[]{:S(2)}, u32[]{:S(2)}) async-start(bf16[64,15,1024]{2,1,0:T(8,128)(2,1)} %reshape.219), calls=%async_computation | async-start | bytes 4194304 | tf_op jit(solution)/shard_map/all_to_all | solution.py:94
  83.5 1.4 slice.60
  85.0 3.7 reshape.229
  88.7 43.9 %all-to-all-done = bf16[64,15,1024]{2,1,0:T(8,128)(2,1)} async-done(((bf16[64,15,1024]{2,1,0:T(8,128)(2,1)}), bf16[64,15,1024]{2,1,0:T(8,128)(2,1)}, u32[]{:S(2)}, u32[]{:S(2)}) %all-to-all-start) | async-done | bytes 1966112 | tf_op jit(solution)/shard_map/all_to_all | solution.py:94
  132.7 8.0 %all-to-all-start.3 = ((bf16[64,15,1024]{2,1,0:T(8,128)(2,1)}), bf16[64,15,1024]{2,1,0:T(8,128)(2,1)}, u32[]{:S(2)}, u32[]{:S(2)}) async-start(bf16[64,15,1024]{2,1,0:T(8,128)(2,1)} %reshape.229), calls=%async_computation.3 | async-start | bytes 4194304 | tf_op jit(solution)/shard_map/all_to_all | solution.py:95
  140.7 34.4 %all_gather.27 = bf16[1,1024,384]{2,1,0:T(8,128)(2,1)} all-gather(bf16[1,128,384]{2,1,0:T(8,128)(2,1)S(1)} %copy-done.11), channel_id=1, replica_groups=mesh['dp'=8,'expert'=64] {'dp'}, dimensions={1}, use_global_device_ids=true | all-gather | bytes 884736 | tf_op jit(solution)/shard_map/all_gather | solution.py:101
  175.2 26.3 %all_gather.28 = bf16[1,1024,384]{2,1,0:T(8,128)(2,1)S(1)} all-gather(bf16[1,128,384]{2,1,0:T(8,128)(2,1)S(1)} %copy-done.9), channel_id=1, replica_groups=mesh['dp'=8,'expert'=64] {'dp'}, dimensions={1}, use_global_device_ids=true | all-gather | bytes 884736 | tf_op jit(solution)/shard_map/all_gather | solution.py:102
  201.5 27.0 %all_gather.29 = bf16[1,384,1024]{2,1,0:T(8,128)(2,1)} all-gather(bf16[1,384,128]{2,1,0:T(8,128)(2,1)S(1)} %copy-done.10), channel_id=1, replica_groups=mesh['dp'=8,'expert'=64] {'dp'}, dimensions={2}, use_global_device_ids=true | all-gather | bytes 884736 | tf_op jit(solution)/shard_map/all_gather | solution.py:103
  228.5 3.7 reshape.220
  232.2 3.0 fusion.16
  236.5 1.2 copy-done.22
  237.7 2.5 convolution_convert_fusion
  240.2 3.8 reshape_transpose_reshape.8
  244.0 10.4 %all-to-all-start.1 = ((bf16[64,15,1024]{2,1,0:T(8,128)(2,1)}), bf16[64,15,1024]{2,1,0:T(8,128)(2,1)}, u32[]{:S(2)}, u32[]{:S(2)}) async-start(bf16[64,15,1024]{2,1,0:T(8,128)(2,1)} %reshape_transpose_reshape.8), calls=%async_computation.1 | async-start | bytes 4194304 | tf_op jit(solution)/shard_map/all_to_all | solution.py:135
  254.5 1.3 fusion.49
  262.7 193.6 %all-reduce.3.cloned.1.call-done = (bf16[384,128]{1,0:T(8,128)(2,1)}, bf16[384,128]{1,0:T(8,128)(2,1)}, bf16[128,384]{1,0:T(8,128)(2,1)}, bf16[128,384]{1,0:T(8,...) async-done(((bf16[384,128]{1,0:T(8,128)(2,1)}, bf16[384,128]{1,0:T(8,128)(2,1)}, bf16[128,384]{1,0:T(8,128)(2,1)}, bf16[128,384]{1,0:T(8,128)(2,1)}, ...) | async-done | bytes 589840 | tf_op jit(solution)/shard_map/psum | solution.py:11
  456.2 30.5 %all_gather.31 = bf16[1024,384]{1,0:T(8,128)(2,1)} all-gather(bf16[128,384]{1,0:T(8,128)(2,1)} %get-tuple-element.17), channel_id=1, replica_groups=mesh['dp'=8,'expert'=64] {'dp'}, dimensions={0}, use_global_device_ids=true | all-gather | bytes 884736 | tf_op jit(solution)/shard_map/all_gather | solution.py:120
  486.7 2.6 reshape.230
  489.4 2.5 convolution_multiply_fusion
  491.9 1.5 fusion.14
  493.4 1.2 add_convert_fusion
  494.6 1.6 reshape_transpose_reshape.9
  496.3 11.2 %all-to-all-start.4 = ((bf16[64,15,1024]{2,1,0:T(8,128)(2,1)}), bf16[64,15,1024]{2,1,0:T(8,128)(2,1)}, u32[]{:S(2)}, u32[]{:S(2)}) async-start(bf16[64,15,1024]{2,1,0:T(8,128)(2,1)} %reshape_transpose_reshape.9), calls=%async_computation.4 | async-start | bytes 4194304 | tf_op jit(solution)/shard_map/all_to_all | solution.py:142
  507.5 26.3 %all_gather.30 = bf16[1024,384]{1,0:T(8,128)(2,1)S(1)} all-gather(bf16[128,384]{1,0:T(8,128)(2,1)S(1)} %copy-done.17), channel_id=1, replica_groups=mesh['dp'=8,'expert'=64] {'dp'}, dimensions={0}, use_global_device_ids=true | all-gather | bytes 884736 | tf_op jit(solution)/shard_map/all_gather | solution.py:120
  534.2 26.2 %all_gather.33 = bf16[1024,384]{1,0:T(8,128)(2,1)S(1)} all-gather(bf16[128,384]{1,0:T(8,128)(2,1)S(1)} %copy-done.16), channel_id=1, replica_groups=mesh['dp'=8,'expert'=64] {'dp'}, dimensions={0}, use_global_device_ids=true | all-gather | bytes 884736 | tf_op jit(solution)/shard_map/all_gather | solution.py:121
  560.4 26.4 %all_gather.32 = bf16[1024,384]{1,0:T(8,128)(2,1)S(1)} all-gather(bf16[128,384]{1,0:T(8,128)(2,1)S(1)} %copy-done.15), channel_id=1, replica_groups=mesh['dp'=8,'expert'=64] {'dp'}, dimensions={0}, use_global_device_ids=true | all-gather | bytes 884736 | tf_op jit(solution)/shard_map/all_gather | solution.py:121
  587.3 26.7 %all_gather.35 = bf16[384,1024]{1,0:T(8,128)(2,1)S(1)} all-gather(bf16[384,128]{1,0:T(8,128)(2,1)S(1)} %copy-done.14), channel_id=1, replica_groups=mesh['dp'=8,'expert'=64] {'dp'}, dimensions={1}, use_global_device_ids=true | all-gather | bytes 884736 | tf_op jit(solution)/shard_map/all_gather | solution.py:122
  614.0 24.3 %all_gather.34 = bf16[384,1024]{1,0:T(8,128)(2,1)S(1)} all-gather(bf16[384,128]{1,0:T(8,128)(2,1)S(1)} %copy-done.13), channel_id=1, replica_groups=mesh['dp'=8,'expert'=64] {'dp'}, dimensions={1}, use_global_device_ids=true | all-gather | bytes 884736 | tf_op jit(solution)/shard_map/all_gather | solution.py:122
  640.8 3.8 reshape.224
  644.6 1.7 pad_maximum_fusion
  646.3 5.4 gather_fusion
  651.7 2.4 fusion.2
  654.9 1.3 fusion
  656.9 3.7 reshape.231
  660.7 1.7 pad_maximum_fusion.1
  662.4 5.4 gather_fusion.2
  667.8 3.7 bitcast_reduce_fusion
  (106 shorter events, 17.8 us)
Async XLA Ops:
  7.2 49.2 %copy-start = (bf16[128,1024]{1,0:T(8,128)(2,1)S(1)}, bf16[128,1024]{1,0:T(8,128)(2,1)}, u32[]{:S(2)}) copy-start(bf16[128,1024]{1,0:T(8,128)(2,1)} %param.10) | copy-start | bytes 786436
  31.4 0.5 copy-start.19
  41.4 30.9 %all-to-all-start.2 = ((bf16[64,1,15]{2,1,0:T(2,128)(2,1)}), bf16[64,1,15]{2,1,0:T(2,128)(2,1)S(1)}, u32[]{:S(2)}, u32[]{:S(2)}) async-start(bf16[64,1,15]{2,1,0:T(2,128)(2,1)} %convert_element_type.86), calls=%async_computation.2 | async-start | bytes 65536 | tf_op jit(solution)/shard_map/all_to_all | solution.py:96
  56.4 4.4 copy-start.1
  69.1 1.4 copy-start.2
  72.3 11.3 %copy-start.3 = (bf16[1072,1024]{1,0:T(8,128)(2,1)S(1)}, bf16[1072,1024]{1,0:T(8,128)(2,1)}, u32[]{:S(2)}) copy-start(bf16[1072,1024]{1,0:T(8,128)(2,1)} %get-tuple-element.25) | copy-start | bytes 6586372
  72.3 0.6 copy-start.12
  72.9 59.8 %all-to-all-start = ((bf16[64,15,1024]{2,1,0:T(8,128)(2,1)}), bf16[64,15,1024]{2,1,0:T(8,128)(2,1)}, u32[]{:S(2)}, u32[]{:S(2)}) async-start(bf16[64,15,1024]{2,1,0:T(8,128)(2,1)} %reshape.219), calls=%async_computation | async-start | bytes 4194304 | tf_op jit(solution)/shard_map/all_to_all | solution.py:94
  88.7 52.0 %copy-start.11 = (bf16[1,128,384]{2,1,0:T(8,128)(2,1)S(1)}, bf16[1,128,384]{2,1,0:T(8,128)(2,1)}, u32[]{:S(2)}) copy-start(bf16[1,128,384]{2,1,0:T(8,128)(2,1)} %param.13) | copy-start | bytes 294916
  88.7 86.5 %copy-start.9 = (bf16[1,128,384]{2,1,0:T(8,128)(2,1)S(1)}, bf16[1,128,384]{2,1,0:T(8,128)(2,1)}, u32[]{:S(2)}) copy-start(bf16[1,128,384]{2,1,0:T(8,128)(2,1)} %param.14) | copy-start | bytes 294916
  88.7 112.8 %copy-start.10 = (bf16[1,384,128]{2,1,0:T(8,128)(2,1)S(1)}, bf16[1,384,128]{2,1,0:T(8,128)(2,1)}, u32[]{:S(2)}) copy-start(bf16[1,384,128]{2,1,0:T(8,128)(2,1)} %param.15) | copy-start | bytes 294916
  132.7 111.3 %all-to-all-start.3 = ((bf16[64,15,1024]{2,1,0:T(8,128)(2,1)}), bf16[64,15,1024]{2,1,0:T(8,128)(2,1)}, u32[]{:S(2)}, u32[]{:S(2)}) async-start(bf16[64,15,1024]{2,1,0:T(8,128)(2,1)} %reshape.229), calls=%async_computation.3 | async-start | bytes 4194304 | tf_op jit(solution)/shard_map/all_to_all | solution.py:95
  232.2 3.0 copy-start.5
  235.3 1.2 copy-start.20
  235.3 2.4 copy-start.7
  236.5 1.2 copy-start.22
  244.0 252.3 %all-to-all-start.1 = ((bf16[64,15,1024]{2,1,0:T(8,128)(2,1)}), bf16[64,15,1024]{2,1,0:T(8,128)(2,1)}, u32[]{:S(2)}, u32[]{:S(2)}) async-start(bf16[64,15,1024]{2,1,0:T(8,128)(2,1)} %reshape_transpose_reshape.8), calls=%async_computation.1 | async-start | bytes 4194304 | tf_op jit(solution)/shard_map/all_to_all | solution.py:135
  254.4 6.4 copy-start.18
  254.4 201.8 %all-reduce.3.cloned.1.call-start = ((), (), s32[]{:S(2)}) async-start(), calls=%async_computation.5 | async-start | bytes 1179648 | tf_op jit(solution)/shard_map/psum | solution.py:11
  489.3 2.5 copy-start.6
  489.4 2.5 copy-start.21
  489.4 2.5 copy-start.23
  496.3 11.3 %copy-start.17 = (bf16[128,384]{1,0:T(8,128)(2,1)S(1)}, bf16[128,384]{1,0:T(8,128)(2,1)}, u32[]{:S(2)}) copy-start(bf16[128,384]{1,0:T(8,128)(2,1)} %get-tuple-element.18) | copy-start | bytes 294916
  496.3 37.6 %copy-start.8 = (bf16[1024,384]{1,0:T(8,128)(2,1)S(1)}, bf16[1024,384]{1,0:T(8,128)(2,1)}, u32[]{:S(2)}) copy-start(bf16[1024,384]{1,0:T(8,128)(2,1)} %all_gather.31) | copy-start | bytes 2359300
  496.3 160.6 %all-to-all-start.4 = ((bf16[64,15,1024]{2,1,0:T(8,128)(2,1)}), bf16[64,15,1024]{2,1,0:T(8,128)(2,1)}, u32[]{:S(2)}, u32[]{:S(2)}) async-start(bf16[64,15,1024]{2,1,0:T(8,128)(2,1)} %reshape_transpose_reshape.9), calls=%async_computation.4 | async-start | bytes 4194304 | tf_op jit(solution)/shard_map/all_to_all | solution.py:142
  507.5 26.7 %copy-start.16 = (bf16[128,384]{1,0:T(8,128)(2,1)S(1)}, bf16[128,384]{1,0:T(8,128)(2,1)}, u32[]{:S(2)}) copy-start(bf16[128,384]{1,0:T(8,128)(2,1)} %get-tuple-element.15) | copy-start | bytes 294916
  533.8 26.6 %copy-start.15 = (bf16[128,384]{1,0:T(8,128)(2,1)S(1)}, bf16[128,384]{1,0:T(8,128)(2,1)}, u32[]{:S(2)}) copy-start(bf16[128,384]{1,0:T(8,128)(2,1)} %get-tuple-element.16) | copy-start | bytes 294916
  560.4 26.9 %copy-start.14 = (bf16[384,128]{1,0:T(8,128)(2,1)S(1)}, bf16[384,128]{1,0:T(8,128)(2,1)}, u32[]{:S(2)}) copy-start(bf16[384,128]{1,0:T(8,128)(2,1)} %get-tuple-element.13) | copy-start | bytes 294916
  586.8 27.1 %copy-start.13 = (bf16[384,128]{1,0:T(8,128)(2,1)S(1)}, bf16[384,128]{1,0:T(8,128)(2,1)}, u32[]{:S(2)}) copy-start(bf16[384,128]{1,0:T(8,128)(2,1)} %get-tuple-element.14) | copy-start | bytes 294916
  651.7 3.2 copy-start.4
Sparse Core Ops, SparseCore 0:
  259.9 196.3 all-reduce.2
where the time goes:
time: 680 us; the launch traced here: 678 us
  blocking collectives  248 us (36%)
  waiting for transfers between devices  238 us (35%)
  local copies, waits for them, and re-layouts  71.4 us (11%)
  starting transfers between devices  51 us (8%)
  other arithmetic  35.4 us (5%)
  matrix products  19 us (3%)
  between operations  15.9 us (2%)
    psum x1, waiting for transfers between devices, broadcast(): return lax.psum(block, axis)  194 us
    all_gather x2, blocking collectives, on_device(): lax.all_gather(shard_gate, 'dp', axis=0, tiled=True)  56.8 us
    all_gather x2, blocking collectives, on_device(): lax.all_gather(shard_up, 'dp', axis=0, tiled=True)  52.6 us
    all_gather x2, blocking collectives, on_device(): lax.all_gather(shard_down, 'dp', axis=1, tiled=True)  51 us
    all_to_all x1, waiting for transfers between devices, on_device(): lax.all_to_all(send_x, 'expert', split_axis=0, concat_axis=0, tiled=True)  43.9 us
    all_gather x1, blocking collectives, on_device(): lax.all_gather(w_gate, 'dp', axis=1, tiled=True)  34.4 us
    all_gather x1, blocking collectives, on_device(): lax.all_gather(w_down, 'dp', axis=2, tiled=True)  27 us
    all_gather x1, blocking collectives, on_device(): lax.all_gather(w_up, 'dp', axis=1, tiled=True)  26.3 us
  transfers between devices with their start and end apart: 6, of which 2 were waited for; matrix products, arithmetic and copies ran while one was open for 11% of the time, Pallas kernels for 0%

commit v1 on v0

--- a/solution.py
+++ b/solution.py
@@ -8,7 +8,7 @@
 
 def broadcast(block, axis, owner):
     block = jnp.where(lax.axis_index(axis) == owner, block, jnp.zeros_like(block))
-    return lax.psum(block, axis)
+    return jnp.sum(lax.all_gather(block, axis), axis=0)
 
 
 def to_owner(array, owners, local_count):

time: 680 us -> 725 us (1.066)
  the two profiles are of different devices: /device:TPU:22 before, /device:TPU:4 now
where the time goes in v1:
time: 725 us; the launch traced here: 723 us
  waiting for transfers between devices  257 us (35%)
  blocking collectives  247 us (34%)
  local copies, waits for them, and re-layouts  74.6 us (10%)
  other arithmetic  55.3 us (8%)
  starting transfers between devices  51.6 us (7%)
  matrix products  21.8 us (3%)
  between operations  16 us (2%)
    all_gather x6, waiting for transfers between devices, broadcast(): return jnp.sum(lax.all_gather(block, axis), axis=0)  111 us
    all_to_all x1, waiting for transfers between devices, on_device(): lax.all_to_all(send_x, 'expert', split_axis=0, concat_axis=0, tiled=True)  57.4 us
    all_gather x2, blocking collectives, on_device(): lax.all_gather(shard_gate, 'dp', axis=0, tiled=True)  54.6 us
    all_gather x2, blocking collectives, on_device(): lax.all_gather(shard_down, 'dp', axis=1, tiled=True)  52.5 us
    all_gather x2, blocking collectives, on_device(): lax.all_gather(shard_up, 'dp', axis=0, tiled=True)  52.4 us
    all_to_all x1, waiting for transfers between devices, on_device(): lax.all_to_all(from_owner(row_grad, owners, local_count), 'expert', split...  44.9 us
    all_to_all x1, waiting for transfers between devices, on_device(): lax.all_to_all(from_owner(expert_out, owners, local_count), 'expert', spl...  42.4 us
    all_gather x1, blocking collectives, on_device(): lax.all_gather(w_gate, 'dp', axis=1, tiled=True)  34.3 us
  transfers between devices with their start and end apart: 11, of which 5 were waited for; matrix products, arithmetic and copies ran while one was open for 13% of the time, Pallas kernels for 0%

profile of v1, /device:TPU:4, one launch (start us, length us, event | category | flops | bytes accessed | tf_op | source)
XLA Modules:
  0.0 723.0 jit_solution(3519056120360197153)
XLA Ops:
  8.4 18.0 %reduce-window.6 = s32[64,8,128]{2,1,0:T(8,128)S(1)} reduce-window(s32[64,8,128]{2,1,0:T(8,128)S(1)} %fusion.22, s32[]{:T(128)} %constant.111.clone.1), window={size=1x1x128 pad=0_0x0_0x127_0}, to_apply=%region_5.6 | reduce-window | flops 8323072 | bytes 524292 | tf_op jit(solution)/shard_map/reduce-window
  27.1 2.0 top_k.11
  35.9 4.3 scatter_custom_fusion.1
  40.3 4.4 gather_fusion.1
  45.5 10.7 %all-to-all-start.2 = ((bf16[64,1,15]{2,1,0:T(2,128)(2,1)}), bf16[64,1,15]{2,1,0:T(2,128)(2,1)S(1)}, u32[]{:S(2)}, u32[]{:S(2)}) async-start(bf16[64,1,15]{2,1,0:T(2,128)(2,1)} %convert_element_type.98), calls=%async_computation.2 | async-start | bytes 65536 | tf_op jit(solution)/shard_map/all_to_all | solution.py:96
  56.2 4.3 scatter_custom_fusion
  60.6 4.4 gather_fusion.4
  65.0 4.9 gather_fusion.3
  69.9 3.3 broadcast_select_fusion
  76.4 10.7 %all-to-all-start = ((bf16[64,15,1024]{2,1,0:T(8,128)(2,1)}), bf16[64,15,1024]{2,1,0:T(8,128)(2,1)}, u32[]{:S(2)}, u32[]{:S(2)}) async-start(bf16[64,15,1024]{2,1,0:T(8,128)(2,1)} %reshape.201), calls=%async_computation | async-start | bytes 4194304 | tf_op jit(solution)/shard_map/all_to_all | solution.py:94
  88.5 3.7 reshape.211
  92.2 57.4 %all-to-all-done = bf16[64,15,1024]{2,1,0:T(8,128)(2,1)} async-done(((bf16[64,15,1024]{2,1,0:T(8,128)(2,1)}), bf16[64,15,1024]{2,1,0:T(8,128)(2,1)}, u32[]{:S(2)}, u32[]{:S(2)}) %all-to-all-start) | async-done | bytes 1966112 | tf_op jit(solution)/shard_map/all_to_all | solution.py:94
  149.6 9.4 %all-to-all-start.3 = ((bf16[64,15,1024]{2,1,0:T(8,128)(2,1)}), bf16[64,15,1024]{2,1,0:T(8,128)(2,1)}, u32[]{:S(2)}, u32[]{:S(2)}) async-start(bf16[64,15,1024]{2,1,0:T(8,128)(2,1)} %reshape.211), calls=%async_computation.3 | async-start | bytes 4194304 | tf_op jit(solution)/shard_map/all_to_all | solution.py:95
  159.5 34.3 %all_gather.51 = bf16[1,1024,384]{2,1,0:T(8,128)(2,1)} all-gather(bf16[1,128,384]{2,1,0:T(8,128)(2,1)S(1)} %copy-done.10), channel_id=1, replica_groups=mesh['dp'=8,'expert'=64] {'dp'}, dimensions={1}, use_global_device_ids=true | all-gather | bytes 884736 | tf_op jit(solution)/shard_map/all_gather | solution.py:101
  193.8 26.2 %all_gather.52 = bf16[1,1024,384]{2,1,0:T(8,128)(2,1)S(1)} all-gather(bf16[1,128,384]{2,1,0:T(8,128)(2,1)S(1)} %copy-done.11), channel_id=1, replica_groups=mesh['dp'=8,'expert'=64] {'dp'}, dimensions={1}, use_global_device_ids=true | all-gather | bytes 884736 | tf_op jit(solution)/shard_map/all_gather | solution.py:102
  220.0 26.7 %all_gather.53 = bf16[1,384,1024]{2,1,0:T(8,128)(2,1)} all-gather(bf16[1,384,128]{2,1,0:T(8,128)(2,1)S(1)} %copy-done.12), channel_id=1, replica_groups=mesh['dp'=8,'expert'=64] {'dp'}, dimensions={2}, use_global_device_ids=true | all-gather | bytes 884736 | tf_op jit(solution)/shard_map/all_gather | solution.py:103
  246.7 3.8 reshape.202
  250.4 3.0 fusion.16
  255.9 2.5 convolution_convert_fusion
  258.4 3.7 reshape_transpose_reshape.8
  262.1 11.2 %all-to-all-start.1 = ((bf16[64,15,1024]{2,1,0:T(8,128)(2,1)}), bf16[64,15,1024]{2,1,0:T(8,128)(2,1)}, u32[]{:S(2)}, u32[]{:S(2)}) async-start(bf16[64,15,1024]{2,1,0:T(8,128)(2,1)} %reshape_transpose_reshape.8), calls=%async_computation.1 | async-start | bytes 4194304 | tf_op jit(solution)/shard_map/all_to_all | solution.py:135
  273.6 3.8 reshape.212
  277.3 3.1 convolution_multiply_fusion
  282.0 2.5 add_convert_fusion
  284.5 3.7 reshape_transpose_reshape.9
  288.2 42.4 %all-to-all-done.1 = bf16[64,15,1024]{2,1,0:T(8,128)(2,1)} async-done(((bf16[64,15,1024]{2,1,0:T(8,128)(2,1)}), bf16[64,15,1024]{2,1,0:T(8,128)(2,1)}, u32[]{:S(2)}, u32[]{:S(2)}) %all-to-all-start.1) | async-done | bytes 1966112 | tf_op jit(solution)/shard_map/all_to_all | solution.py:135
  330.6 9.4 %all-to-all-start.4 = ((bf16[64,15,1024]{2,1,0:T(8,128)(2,1)}), bf16[64,15,1024]{2,1,0:T(8,128)(2,1)}, u32[]{:S(2)}, u32[]{:S(2)}) async-start(bf16[64,15,1024]{2,1,0:T(8,128)(2,1)} %reshape_transpose_reshape.9), calls=%async_computation.4 | async-start | bytes 4194304 | tf_op jit(solution)/shard_map/all_to_all | solution.py:142
  343.2 3.8 reshape.206
  347.0 44.9 %all-to-all-done.4 = bf16[64,15,1024]{2,1,0:T(8,128)(2,1)} async-done(((bf16[64,15,1024]{2,1,0:T(8,128)(2,1)}), bf16[64,15,1024]{2,1,0:T(8,128)(2,1)}, u32[]{:S(2)}, u32[]{:S(2)}) %all-to-all-start.4) | async-done | bytes 1966112 | tf_op jit(solution)/shard_map/all_to_all | solution.py:142
  391.9 3.7 reshape.213
  395.6 3.8 reduce_sum.123
  399.4 3.8 reduce_sum.124
  403.2 4.1 reduce_sum.125
  407.3 27.9 %all-gather.7.cloned.1.call-done = bf16[64,128,384]{2,1,0:T(8,128)(2,1)} async-done(((bf16[1,128,384]{2,1,0:T(8,128)(2,1)}), bf16[64,128,384]{2,1,0:T(8,128)(2,1)}) %all-gather.7.cloned.1.call-update) | async-done | bytes 6291472 | tf_op jit(solution)/shard_map/all_gather | solution.py:11
  435.2 3.8 reduce_sum.120
  439.0 82.7 %all-gather.9.cloned.1.call-done = bf16[64,128,384]{2,1,0:T(8,128)(2,1)} async-done(((bf16[1,128,384]{2,1,0:T(8,128)(2,1)}), bf16[64,128,384]{2,1,0:T(8,128)(2,1)}) %all-gather.9.cloned.1.call-update) | async-done | bytes 6291472 | tf_op jit(solution)/shard_map/all_gather | solution.py:11
  521.7 3.8 reduce_sum.121
  525.5 28.3 %all_gather.57 = bf16[1024,384]{1,0:T(8,128)(2,1)S(1)} all-gather(bf16[128,384]{1,0:T(8,128)(2,1)S(1)} %reduce_sum.121), channel_id=1, replica_groups=mesh['dp'=8,'expert'=64] {'dp'}, dimensions={0}, use_global_device_ids=true | all-gather | bytes 884736 | tf_op jit(solution)/shard_map/all_gather | solution.py:120
  553.8 26.3 %all_gather.55 = bf16[1024,384]{1,0:T(8,128)(2,1)S(1)} all-gather(bf16[128,384]{1,0:T(8,128)(2,1)S(1)} %reduce_sum.120), channel_id=1, replica_groups=mesh['dp'=8,'expert'=64] {'dp'}, dimensions={0}, use_global_device_ids=true | all-gather | bytes 884736 | tf_op jit(solution)/shard_map/all_gather | solution.py:120
  580.1 25.4 %all_gather.65 = bf16[384,1024]{1,0:T(8,128)(2,1)S(1)} all-gather(bf16[384,128]{1,0:T(8,128)(2,1)S(1)} %reduce_sum.125), channel_id=1, replica_groups=mesh['dp'=8,'expert'=64] {'dp'}, dimensions={1}, use_global_device_ids=true | all-gather | bytes 884736 | tf_op jit(solution)/shard_map/all_gather | solution.py:122
  605.5 27.1 %all_gather.63 = bf16[384,1024]{1,0:T(8,128)(2,1)} all-gather(bf16[384,128]{1,0:T(8,128)(2,1)S(1)} %reduce_sum.124), channel_id=1, replica_groups=mesh['dp'=8,'expert'=64] {'dp'}, dimensions={1}, use_global_device_ids=true | all-gather | bytes 884736 | tf_op jit(solution)/shard_map/all_gather | solution.py:122
  632.6 26.3 %all_gather.61 = bf16[1024,384]{1,0:T(8,128)(2,1)S(1)} all-gather(bf16[128,384]{1,0:T(8,128)(2,1)S(1)} %reduce_sum.123), channel_id=1, replica_groups=mesh['dp'=8,'expert'=64] {'dp'}, dimensions={0}, use_global_device_ids=true | all-gather | bytes 884736 | tf_op jit(solution)/shard_map/all_gather | solution.py:121
  658.9 3.8 reduce_sum.122
  662.7 26.1 %all_gather.59 = bf16[1024,384]{1,0:T(8,128)(2,1)S(1)} all-gather(bf16[128,384]{1,0:T(8,128)(2,1)S(1)} %reduce_sum.122), channel_id=1, replica_groups=mesh['dp'=8,'expert'=64] {'dp'}, dimensions={0}, use_global_device_ids=true | all-gather | bytes 884736 | tf_op jit(solution)/shard_map/all_gather | solution.py:121
  694.8 5.4 gather_fusion
  700.2 3.0 fusion
  707.0 5.4 gather_fusion.2
  712.4 3.7 bitcast_reduce_fusion
  (123 shorter events, 30.4 us)
Async XLA Ops:
  7.2 53.4 %copy-start = (bf16[128,1024]{1,0:T(8,128)(2,1)S(1)}, bf16[128,1024]{1,0:T(8,128)(2,1)}, u32[]{:S(2)}) copy-start(bf16[128,1024]{1,0:T(8,128)(2,1)} %param.10) | copy-start | bytes 786436
  7.2 24.5 %copy-start.11 = (bf16[1,128,384]{2,1,0:T(8,128)(2,1)S(1)}, bf16[1,128,384]{2,1,0:T(8,128)(2,1)}, u32[]{:S(2)}) copy-start(bf16[1,128,384]{2,1,0:T(8,128)(2,1)} %param.14) | copy-start | bytes 294916
  7.2 25.2 %copy-start.12 = (bf16[1,384,128]{2,1,0:T(8,128)(2,1)S(1)}, bf16[1,384,128]{2,1,0:T(8,128)(2,1)}, u32[]{:S(2)}) copy-start(bf16[1,384,128]{2,1,0:T(8,128)(2,1)} %param.15) | copy-start | bytes 294916
  7.2 26.8 %copy-start.10 = (bf16[1,128,384]{2,1,0:T(8,128)(2,1)S(1)}, bf16[1,128,384]{2,1,0:T(8,128)(2,1)}, u32[]{:S(2)}) copy-start(bf16[1,128,384]{2,1,0:T(8,128)(2,1)} %param.13) | copy-start | bytes 294916
  7.2 388.4 %all-gather.13.cloned.1.call-start = ((), (), s32[]{:S(2)}) async-start(), calls=%async_computation.8 | async-start | bytes 6389760 | tf_op jit(solution)/shard_map/all_gather | solution.py:11
  8.3 27.0 %copy-start.17 = (s32[128,8]{0,1:T(8,128)S(1)}, s32[128,8]{0,1:T(8,128)}, u32[]{:S(2)}) copy-start(s32[128,8]{0,1:T(8,128)} %param.11) | copy-start | bytes 12292
  8.3 27.2 %copy-start.16 = (f32[128,8]{0,1:T(8,128)S(1)}, f32[128,8]{0,1:T(8,128)}, u32[]{:S(2)}) copy-start(f32[128,8]{0,1:T(8,128)} %param.12) | copy-start | bytes 12292
  32.4 367.0 %all-gather.15.cloned.1.call-start = ((), (), s32[]{:S(2)}) async-start(), calls=%async_computation.9 | async-start | bytes 6389760 | tf_op jit(solution)/shard_map/all_gather | solution.py:11
  33.2 370.1 %all-gather.17.cloned.1.call-start = ((), (), s32[]{:S(2)}) async-start(), calls=%async_computation.10 | async-start | bytes 6389760 | tf_op jit(solution)/shard_map/all_gather | solution.py:11
  33.9 401.3 %all-gather.7.cloned.1.call-start = ((), (), s32[]{:S(2)}) async-start(), calls=%async_computation.5 | async-start | bytes 6389760 | tf_op jit(solution)/shard_map/all_gather | solution.py:11
  34.7 487.0 %all-gather.9.cloned.1.call-start = ((), (), s32[]{:S(2)}) async-start(), calls=%async_computation.6 | async-start | bytes 6389760 | tf_op jit(solution)/shard_map/all_gather | solution.py:11
  45.5 30.9 %all-to-all-start.2 = ((bf16[64,1,15]{2,1,0:T(2,128)(2,1)}), bf16[64,1,15]{2,1,0:T(2,128)(2,1)S(1)}, u32[]{:S(2)}, u32[]{:S(2)}) async-start(bf16[64,1,15]{2,1,0:T(2,128)(2,1)} %convert_element_type.98), calls=%async_computation.2 | async-start | bytes 65536 | tf_op jit(solution)/shard_map/all_to_all | solution.py:96
  60.6 4.4 copy-start.1
  73.2 1.3 copy-start.2
  76.4 10.7 %copy-start.3 = (bf16[1072,1024]{1,0:T(8,128)(2,1)S(1)}, bf16[1072,1024]{1,0:T(8,128)(2,1)}, u32[]{:S(2)}) copy-start(bf16[1072,1024]{1,0:T(8,128)(2,1)} %get-tuple-element.19) | copy-start | bytes 6586372
  76.4 73.2 %all-to-all-start = ((bf16[64,15,1024]{2,1,0:T(8,128)(2,1)}), bf16[64,15,1024]{2,1,0:T(8,128)(2,1)}, u32[]{:S(2)}, u32[]{:S(2)}) async-start(bf16[64,15,1024]{2,1,0:T(8,128)(2,1)} %reshape.201), calls=%async_computation | async-start | bytes 4194304 | tf_op jit(solution)/shard_map/all_to_all | solution.py:94
  149.6 112.5 %all-to-all-start.3 = ((bf16[64,15,1024]{2,1,0:T(8,128)(2,1)}), bf16[64,15,1024]{2,1,0:T(8,128)(2,1)}, u32[]{:S(2)}, u32[]{:S(2)}) async-start(bf16[64,15,1024]{2,1,0:T(8,128)(2,1)} %reshape.211), calls=%async_computation.3 | async-start | bytes 4194304 | tf_op jit(solution)/shard_map/all_to_all | solution.py:95
  159.0 499.9 %all-gather.11.cloned.1.call-start = ((), (), s32[]{:S(2)}) async-start(), calls=%async_computation.7 | async-start | bytes 6389760 | tf_op jit(solution)/shard_map/all_gather | solution.py:11
  250.4 3.0 copy-start.6
  253.5 1.2 copy-start.18
  253.5 2.4 copy-start.8
  254.7 1.2 copy-start.20
  262.1 68.5 %all-to-all-start.1 = ((bf16[64,15,1024]{2,1,0:T(8,128)(2,1)}), bf16[64,15,1024]{2,1,0:T(8,128)(2,1)}, u32[]{:S(2)}, u32[]{:S(2)}) async-start(bf16[64,15,1024]{2,1,0:T(8,128)(2,1)} %reshape_transpose_reshape.8), calls=%async_computation.1 | async-start | bytes 4194304 | tf_op jit(solution)/shard_map/all_to_all | solution.py:135
  277.3 3.1 copy-start.7
  277.3 3.1 copy-start.19
  277.3 3.1 copy-start.21
  330.6 61.3 %all-to-all-start.4 = ((bf16[64,15,1024]{2,1,0:T(8,128)(2,1)}), bf16[64,15,1024]{2,1,0:T(8,128)(2,1)}, u32[]{:S(2)}, u32[]{:S(2)}) async-start(bf16[64,15,1024]{2,1,0:T(8,128)(2,1)} %reshape_transpose_reshape.9), calls=%async_computation.4 | async-start | bytes 4194304 | tf_op jit(solution)/shard_map/all_to_all | solution.py:142
  662.7 27.4 %copy-start.15 = (bf16[112,1024]{1,0:T(8,128)(2,1)S(1)}, bf16[112,1024]{1,0:T(8,128)(2,1)}, u32[]{:S(2)}) copy-start(bf16[112,1024]{1,0:T(8,128)(2,1)} %slice.58) | copy-start | bytes 688132
  690.1 1.1 copy-start.9
  690.1 1.2 copy-start.14
  693.1 1.6 copy-start.5
  700.2 3.0 copy-start.4
  700.2 3.0 copy-start.13
Sparse Core Ops, SparseCore 0:
  32.5 116.2 all-gather.12
  152.1 89.3 all-gather.14
  244.8 99.2 all-gather.16
  347.3 87.9 all-gather.6
  438.4 83.2 all-gather.8
  524.9 83.0 all-gather.10
